TPU v7x, 32 devices: a whole 2x2x4 slice. The times are simulated.
32 devices in a mesh: head: 2 (over x), blk: 16 (over z, y, core).
Axes of the slice: x: 2, y: 2, z: 4, core: 2. Of those that a mesh axis runs over, the one named last changes fastest.
Arguments:
- tokens: bfloat16 [16, 256, 768], P('blk', 'head'), may hold values from -6 to 6
- doc_starts: int32 [16], replicated, may hold values from 0 to 4095, as said below
- w_qkv: bfloat16 [768, 2304], P(('head', 'blk')), may hold values from -0.3125 to 0.3125
- b_query: bfloat16 [768], P(('head', 'blk')), may hold values from -3 to 3
- b_value: bfloat16 [768], P(('head', 'blk')), may hold values from -3 to 3
- w_out: bfloat16 [768, 768], P(('head', 'blk')), may hold values from -1.5 to 1.5
- b_out: bfloat16 [768], P(('head', 'blk')), may hold values from -2 to 2
- gain_attn: bfloat16 [768], P(('head', 'blk')), may hold values from 0.5 to 1.5
- shift_attn: bfloat16 [768], P(('head', 'blk')), may hold values from -2 to 2
- w_in: bfloat16 [768, 3072], P(('head', 'blk')), may hold values from -0.21875 to 0.21875
- b_in: bfloat16 [3072], P(('head', 'blk')), may hold values from -3 to 3
- w_down: bfloat16 [3072, 768], P(('head', 'blk')), may hold values from -0.109375 to 0.109375
- b_down: bfloat16 [768], P(('head', 'blk')), may hold values from -2 to 2
- gain_ffn: bfloat16 [768], P(('head', 'blk')), may hold values from 0.5 to 1.5
- shift_ffn: bfloat16 [768], P(('head', 'blk')), may hold values from -2 to 2
- cotangent: bfloat16 [16, 256, 768], P('blk', 'head'), may hold values from -6 to 6
Outputs:
- layer_out: bfloat16 [16, 256, 768], P('blk', 'head')
- grad_tokens: float32 [16, 256, 768], P('blk', 'head')
- grad_w_qkv: float32 [768, 2304], P(('head', 'blk'))
- grad_b_query: float32 [768], P(('head', 'blk'))
- grad_b_value: float32 [768], P(('head', 'blk'))
- grad_w_out: float32 [768, 768], P(('head', 'blk'))
- grad_b_out: float32 [768], P(('head', 'blk'))
- grad_gain_attn: float32 [768], P(('head', 'blk'))
- grad_shift_attn: float32 [768], P(('head', 'blk'))
- grad_w_in: float32 [768, 3072], P(('head', 'blk'))
- grad_b_in: float32 [3072], P(('head', 'blk'))
- grad_w_down: float32 [3072, 768], P(('head', 'blk'))
- grad_b_down: float32 [768], P(('head', 'blk'))
- grad_gain_ffn: float32 [768], P(('head', 'blk'))
- grad_shift_ffn: float32 [768], P(('head', 'blk'))
Inputs may be any that keep to these rules, and one draw needn't show every extreme that they name: `doc_starts`: strictly increasing and the first is 0; a document runs from its start to the next start (the last to the end of the stream); exactly one document has 2304 tokens and every other has fewer.
All inputs are finite; a program needn't handle non-finite values.
Results may differ from a plain program's by a relative error of at most 0.024.
Values may be sent and summed in bfloat16 or wider, within the bound.
No kernel may reach another device: no remote copies, remote signals or barrier semaphores. Data moves between devices by JAX's collectives and lax.ppermute only.
A program may use at most 512 MiB of HBM per device.

v0:
```python
from functools import partial
import math

import jax
import jax.numpy as jnp
from jax import lax
from jax.sharding import PartitionSpec as P

HEADS = 12
HEAD_DIM = 64


masked_score = -1e30
norm_epsilon = 1e-06


def doc_ids(positions, doc_starts):
    return jnp.sum((positions[:, None] >= doc_starts[None, :]).astype(jnp.int32), axis=1) - 1


def normalize(values):
    centered = values - jnp.mean(values, axis=1, keepdims=True)
    inverse_root = lax.rsqrt(jnp.mean(centered * centered, axis=1, keepdims=True) + norm_epsilon)
    return (centered * inverse_root, inverse_root)


def normalize_back(grad_norm, normed, inverse_root):
    return inverse_root * (
        grad_norm
        - jnp.mean(grad_norm, axis=1, keepdims=True)
        - normed * jnp.mean(grad_norm * normed, axis=1, keepdims=True)
    )


def run_blocks(step_fn, running, arrays):
    row_total = arrays[0].shape[0]
    block_width = math.gcd(row_total, 512)
    block_count = row_total // block_width

    def loop_body(block_index, state_now):
        block_parts = tuple(
            (
                lax.dynamic_slice_in_dim(array_item, block_index * block_width, block_width, 0)
                for array_item in arrays
            )
        )
        return step_fn(state_now, block_parts)

    return lax.fori_loop(0, block_count, loop_body, running)


def forward_step(running, block_parts, queries, query_docs, scale_factor):
    run_max, run_sum, accumulated = running
    key_block, value_block, key_docs = block_parts
    piece_rows = key_block.shape[0]
    head_count = queries.shape[1]
    key_three = key_block.reshape(piece_rows, head_count, -1)
    value_three = value_block.reshape(piece_rows, head_count, -1)
    scores = (
        jnp.einsum("qhd,khd->hqk", queries, key_three, preferred_element_type=jnp.float32)
        * scale_factor
    )
    allowed = (query_docs[:, None] == key_docs[None, :])[None]
    new_max = jnp.maximum(run_max, jnp.max(jnp.where(allowed, scores, masked_score), axis=2))
    weights_now = jnp.where(allowed, jnp.exp(scores - new_max[:, :, None]), 0.0)
    factor = jnp.exp(run_max - new_max)
    run_sum = run_sum * factor + jnp.sum(weights_now, axis=2)
    accumulated = accumulated * factor[:, :, None] + jnp.einsum(
        "hqk,khd->hqd",
        weights_now.astype(jnp.bfloat16),
        value_three,
        preferred_element_type=jnp.float32,
    )
    return (new_max, run_sum, accumulated)


def query_grad_step(
    running, block_parts, queries, query_docs, log_sum, grad_three, row_delta, scale_factor
):
    key_block, value_block, key_docs = block_parts
    piece_rows = key_block.shape[0]
    head_count = queries.shape[1]
    key_three = key_block.reshape(piece_rows, head_count, -1)
    value_three = value_block.reshape(piece_rows, head_count, -1)
    scores = (
        jnp.einsum("qhd,khd->hqk", queries, key_three, preferred_element_type=jnp.float32)
        * scale_factor
    )
    allowed = (query_docs[:, None] == key_docs[None, :])[None]
    probability = jnp.where(allowed, jnp.exp(scores - log_sum[:, :, None]), 0.0)
    grad_probs = jnp.einsum(
        "qhd,khd->hqk", grad_three, value_three, preferred_element_type=jnp.float32
    )
    grad_scores = (probability * (grad_probs - row_delta[:, :, None])).astype(jnp.bfloat16)
    return running + jnp.einsum(
        "hqk,khd->hqd", grad_scores, key_three, preferred_element_type=jnp.float32
    )


def key_grad_step(running, block_parts, key_three, value_three, key_docs, scale_factor):
    grad_keys, grad_values = running
    query_block, grad_block, lse_block, delta_block, query_docs = block_parts
    piece_rows = query_block.shape[0]
    head_count = key_three.shape[1]
    query_three = query_block.reshape(piece_rows, head_count, -1)
    grad_three = grad_block.reshape(piece_rows, head_count, -1)
    scores = (
        jnp.einsum("qhd,khd->hqk", query_three, key_three, preferred_element_type=jnp.float32)
        * scale_factor
    )
    allowed = (query_docs[:, None] == key_docs[None, :])[None]
    probability = jnp.where(allowed, jnp.exp(scores - lse_block.T[:, :, None]), 0.0)
    grad_probs = jnp.einsum(
        "qhd,khd->hqk", grad_three, value_three, preferred_element_type=jnp.float32
    )
    grad_scores = (probability * (grad_probs - delta_block.T[:, :, None])).astype(jnp.bfloat16)
    grad_values = grad_values + jnp.einsum(
        "hqk,qhd->khd",
        probability.astype(jnp.bfloat16),
        grad_three,
        preferred_element_type=jnp.float32,
    )
    grad_keys = grad_keys + jnp.einsum(
        "hqk,qhd->khd", grad_scores, query_three, preferred_element_type=jnp.float32
    )
    return (grad_keys, grad_values)


def per_device(
    tokens,
    doc_starts,
    w_qkv,
    b_query,
    b_value,
    w_out,
    b_out,
    gain_attn,
    shift_attn,
    w_in,
    b_in,
    w_down,
    b_down,
    gain_ffn,
    shift_ffn,
    cotangent,
):
    (
        full_qkv,
        full_bquery,
        full_bvalue,
        full_out,
        full_bout,
        full_gain_one,
        full_shift_one,
        full_in,
        full_bin,
        full_down,
        full_bdown,
        full_gain_two,
        full_shift_two,
    ) = (
        lax.all_gather(w_qkv, ("head", "blk"), axis=0, tiled=True),
        lax.all_gather(b_query, ("head", "blk"), axis=0, tiled=True),
        lax.all_gather(b_value, ("head", "blk"), axis=0, tiled=True),
        lax.all_gather(w_out, ("head", "blk"), axis=0, tiled=True),
        lax.all_gather(b_out, ("head", "blk"), axis=0, tiled=True),
        lax.all_gather(gain_attn, ("head", "blk"), axis=0, tiled=True),
        lax.all_gather(shift_attn, ("head", "blk"), axis=0, tiled=True),
        lax.all_gather(w_in, ("head", "blk"), axis=0, tiled=True),
        lax.all_gather(b_in, ("head", "blk"), axis=0, tiled=True),
        lax.all_gather(w_down, ("head", "blk"), axis=0, tiled=True),
        lax.all_gather(b_down, ("head", "blk"), axis=0, tiled=True),
        lax.all_gather(gain_ffn, ("head", "blk"), axis=0, tiled=True),
        lax.all_gather(shift_ffn, ("head", "blk"), axis=0, tiled=True),
    )
    inputs = tokens[0]
    local_rows = inputs.shape[0]
    model_width = inputs.shape[1]
    scale_factor = 1.0 / math.sqrt(HEAD_DIM)
    blk_count = lax.axis_size("blk")
    head_devices = lax.axis_size("head")
    blk_place = lax.axis_index("blk")
    head_place = lax.axis_index("head")
    projected = jnp.dot(inputs, full_qkv, preferred_element_type=jnp.float32)
    query_all = (projected[:, :model_width] + full_bquery.astype(jnp.float32)).astype(jnp.bfloat16)
    key_all = projected[:, model_width : 2 * model_width].astype(jnp.bfloat16)
    value_all = (projected[:, 2 * model_width :] + full_bvalue.astype(jnp.float32)).astype(
        jnp.bfloat16
    )

    def global_rows(linear_rows):
        linear_device = linear_rows // local_rows
        head_part = linear_device // blk_count
        blk_part = linear_device % blk_count
        return (
            blk_part * (head_devices * local_rows)
            + head_part * local_rows
            + linear_rows % local_rows
        )

    query_flat, key_flat, value_flat = (query_all, key_all, value_all)
    group_heads = HEADS
    query_docs = doc_ids(
        global_rows(
            (head_place * blk_count + blk_place) * local_rows + lax.iota(jnp.int32, local_rows)
        ),
        doc_starts,
    )
    query_three = query_flat.reshape(local_rows, group_heads, HEAD_DIM)
    forward_fn = partial(
        forward_step, queries=query_three, query_docs=query_docs, scale_factor=scale_factor
    )
    initial = (
        jnp.full((group_heads, local_rows), masked_score, jnp.float32),
        jnp.zeros((group_heads, local_rows), jnp.float32),
        jnp.zeros((group_heads, local_rows, HEAD_DIM), jnp.float32),
    )
    shard_piece = (
        lax.all_gather(key_flat, ("head", "blk"), axis=0, tiled=True),
        lax.all_gather(value_flat, ("head", "blk"), axis=0, tiled=True),
    )
    piece_rows = shard_piece[0].shape[0]
    key_docs = doc_ids(global_rows(lax.iota(jnp.int32, piece_rows)), doc_starts)
    run_max, run_sum, accumulated = run_blocks(
        forward_fn, initial, (shard_piece[0], shard_piece[1], key_docs)
    )
    log_sum = run_max + jnp.log(run_sum)
    attn_rows = (
        (accumulated / run_sum[:, :, None])
        .transpose(1, 0, 2)
        .reshape(local_rows, group_heads * HEAD_DIM)
    )
    joined = attn_rows.astype(jnp.bfloat16)
    mixed_attn = jnp.dot(joined, full_out, preferred_element_type=jnp.float32)
    resid_one = mixed_attn + full_bout.astype(jnp.float32) + inputs.astype(jnp.float32)
    normed_one, root_one = normalize(resid_one)
    hidden_one = normed_one * full_gain_one.astype(jnp.float32) + full_shift_one.astype(jnp.float32)
    hidden_low = hidden_one.astype(jnp.bfloat16)
    pre_act = jnp.dot(hidden_low, full_in, preferred_element_type=jnp.float32) + full_bin.astype(
        jnp.float32
    )
    activated, gelu_back = jax.vjp(partial(jax.nn.gelu, approximate=True), pre_act)
    act_low = activated.astype(jnp.bfloat16)
    ffn_value = jnp.dot(act_low, full_down, preferred_element_type=jnp.float32)
    resid_two = ffn_value + full_bdown.astype(jnp.float32) + hidden_one
    normed_two, root_two = normalize(resid_two)
    layer_out = (
        normed_two * full_gain_two.astype(jnp.float32) + full_shift_two.astype(jnp.float32)
    ).astype(jnp.bfloat16)
    grad_out = cotangent[0].astype(jnp.float32)
    grad_gain_ffn = jnp.sum(grad_out * normed_two, axis=0)
    grad_shift_ffn = jnp.sum(grad_out, axis=0)
    grad_two = normalize_back(grad_out * full_gain_two.astype(jnp.float32), normed_two, root_two)
    grad_ffn_low = grad_two.astype(jnp.bfloat16)
    grad_b_down = jnp.sum(grad_two, axis=0)
    grad_w_down = jnp.dot(act_low.T, grad_ffn_low, preferred_element_type=jnp.float32)
    grad_act = jnp.dot(grad_ffn_low, full_down.T, preferred_element_type=jnp.float32)
    grad_pre = gelu_back(grad_act)[0].astype(jnp.bfloat16)
    grad_b_in = jnp.sum(grad_pre.astype(jnp.float32), axis=0)
    grad_w_in = jnp.dot(hidden_low.T, grad_pre, preferred_element_type=jnp.float32)
    grad_hidden = jnp.dot(grad_pre, full_in.T, preferred_element_type=jnp.float32) + grad_two
    grad_gain_attn = jnp.sum(grad_hidden * normed_one, axis=0)
    grad_shift_attn = jnp.sum(grad_hidden, axis=0)
    grad_one = normalize_back(grad_hidden * full_gain_one.astype(jnp.float32), normed_one, root_one)
    grad_mix_low = grad_one.astype(jnp.bfloat16)
    grad_b_out = jnp.sum(grad_one, axis=0)
    grad_w_out = jnp.dot(joined.T, grad_mix_low, preferred_element_type=jnp.float32)
    grad_joined = jnp.dot(grad_mix_low, full_out.T, preferred_element_type=jnp.float32).astype(
        jnp.bfloat16
    )
    key_local = key_flat.reshape(local_rows, group_heads, HEAD_DIM)
    value_local = value_flat.reshape(local_rows, group_heads, HEAD_DIM)
    key_fn = partial(
        key_grad_step,
        key_three=key_local,
        value_three=value_local,
        key_docs=query_docs,
        scale_factor=scale_factor,
    )
    zero_keys = (
        jnp.zeros((local_rows, group_heads, HEAD_DIM), jnp.float32),
        jnp.zeros((local_rows, group_heads, HEAD_DIM), jnp.float32),
    )
    grad_three = grad_joined.reshape(local_rows, group_heads, HEAD_DIM)
    row_delta = jnp.sum(
        grad_three.astype(jnp.float32) * attn_rows.reshape(local_rows, group_heads, HEAD_DIM),
        axis=2,
    ).T
    query_fn = partial(
        query_grad_step,
        queries=query_three,
        query_docs=query_docs,
        log_sum=log_sum,
        grad_three=grad_three,
        row_delta=row_delta,
        scale_factor=scale_factor,
    )
    shard_piece = (
        lax.all_gather(key_flat, ("head", "blk"), axis=0, tiled=True),
        lax.all_gather(value_flat, ("head", "blk"), axis=0, tiled=True),
    )
    piece_rows = shard_piece[0].shape[0]
    key_docs = doc_ids(global_rows(lax.iota(jnp.int32, piece_rows)), doc_starts)
    grad_query = run_blocks(
        query_fn,
        jnp.zeros((group_heads, local_rows, HEAD_DIM), jnp.float32),
        (shard_piece[0], shard_piece[1], key_docs),
    )
    lse_every, delta_every = (
        lax.all_gather(log_sum.T, ("head", "blk"), axis=0, tiled=True),
        lax.all_gather(row_delta.T, ("head", "blk"), axis=0, tiled=True),
    )
    shard_piece = (
        lax.all_gather(query_flat, ("head", "blk"), axis=0, tiled=True),
        lax.all_gather(grad_joined, ("head", "blk"), axis=0, tiled=True),
    )
    piece_rows = shard_piece[0].shape[0]
    piece_docs = doc_ids(global_rows(lax.iota(jnp.int32, piece_rows)), doc_starts)
    grad_keys, grad_values = run_blocks(
        key_fn, zero_keys, (shard_piece[0], shard_piece[1], lse_every, delta_every, piece_docs)
    )
    grad_query_all = (
        grad_query.transpose(1, 0, 2).reshape(local_rows, group_heads * HEAD_DIM) * scale_factor
    ).astype(jnp.bfloat16)
    grad_key_all = (grad_keys.reshape(local_rows, group_heads * HEAD_DIM) * scale_factor).astype(
        jnp.bfloat16
    )
    grad_value_all = grad_values.reshape(local_rows, group_heads * HEAD_DIM).astype(jnp.bfloat16)
    grad_qkv = jnp.concatenate([grad_query_all, grad_key_all, grad_value_all], axis=1)
    grad_inputs = grad_one + jnp.dot(grad_qkv, full_qkv.T, preferred_element_type=jnp.float32)
    grad_w_qkv = jnp.dot(inputs.T, grad_qkv, preferred_element_type=jnp.float32)
    grad_b_query = jnp.sum(grad_query_all.astype(jnp.float32), axis=0)
    grad_b_value = jnp.sum(grad_value_all.astype(jnp.float32), axis=0)
    shards = (
        lax.psum_scatter(grad_w_qkv, ("head", "blk"), scatter_dimension=0, tiled=True),
        lax.psum_scatter(grad_b_query, ("head", "blk"), scatter_dimension=0, tiled=True),
        lax.psum_scatter(grad_b_value, ("head", "blk"), scatter_dimension=0, tiled=True),
        lax.psum_scatter(grad_w_out, ("head", "blk"), scatter_dimension=0, tiled=True),
        lax.psum_scatter(grad_b_out, ("head", "blk"), scatter_dimension=0, tiled=True),
        lax.psum_scatter(grad_gain_attn, ("head", "blk"), scatter_dimension=0, tiled=True),
        lax.psum_scatter(grad_shift_attn, ("head", "blk"), scatter_dimension=0, tiled=True),
        lax.psum_scatter(grad_w_in, ("head", "blk"), scatter_dimension=0, tiled=True),
        lax.psum_scatter(grad_b_in, ("head", "blk"), scatter_dimension=0, tiled=True),
        lax.psum_scatter(grad_w_down, ("head", "blk"), scatter_dimension=0, tiled=True),
        lax.psum_scatter(grad_b_down, ("head", "blk"), scatter_dimension=0, tiled=True),
        lax.psum_scatter(grad_gain_ffn, ("head", "blk"), scatter_dimension=0, tiled=True),
        lax.psum_scatter(grad_shift_ffn, ("head", "blk"), scatter_dimension=0, tiled=True),
    )
    return (
        layer_out[None],
        grad_inputs[None],
        shards[0],
        shards[1],
        shards[2],
        shards[3],
        shards[4],
        shards[5],
        shards[6],
        shards[7],
        shards[8],
        shards[9],
        shards[10],
        shards[11],
        shards[12],
    )


def solution(mesh):
    return jax.shard_map(
        per_device,
        mesh=mesh,
        in_specs=(
            P("blk", "head", None),
            P(),
            P(("head", "blk"), None),
            P(("head", "blk")),
            P(("head", "blk")),
            P(("head", "blk"), None),
            P(("head", "blk")),
            P(("head", "blk")),
            P(("head", "blk")),
            P(("head", "blk"), None),
            P(("head", "blk")),
            P(("head", "blk"), None),
            P(("head", "blk")),
            P(("head", "blk")),
            P(("head", "blk")),
            P("blk", "head", None),
        ),
        out_specs=(
            P("blk", "head", None),
            P("blk", "head", None),
            P(("head", "blk"), None),
            P(("head", "blk")),
            P(("head", "blk")),
            P(("head", "blk"), None),
            P(("head", "blk")),
            P(("head", "blk")),
            P(("head", "blk")),
            P(("head", "blk"), None),
            P(("head", "blk")),
            P(("head", "blk"), None),
            P(("head", "blk")),
            P(("head", "blk")),
            P(("head", "blk")),
        ),
        check_vma=False,
    )
```

profile of v0, /device:TPU:0, one launch (start us, length us, event | category | flops | bytes accessed | tf_op | source)
XLA Modules:
  0.0 1065.2 jit_solution(12535656141924638432)
XLA Ops:
  15.5 42.5 %all-reduce.19 = (bf16[768]{0:T(1024)(128)(2,1)S(1)}, bf16[768]{0:T(1024)(128)(2,1)S(1)}, bf16[768]{0:T(1024)(128)(2,1)S(1)}, bf16[768]{0:T(1024)(128)(2,1)S(1)}...) all-reduce(bf16[768]{0:T(1024)(128)(2,1)S(1)} %dynamic-update-slice, ...), channel_id=1, replica_groups=mesh['head'=2,'blk'=16] {'head','blk'}, use_global_device_ids=true, to_apply=%add | all-reduce | flops 9216 | bytes 36864
  58.0 15.8 %all-gather.9.cloned.1.call-done = bf16[768,2304]{1,0:T(8,128)(2,1)} async-done(((bf16[24,2304]{1,0:T(8,128)(2,1)}), bf16[768,2304]{1,0:T(8,128)(2,1)}) %all-gather.9.cloned.1.call-update) | async-done | bytes 3538960 | tf_op jit(solution)/shard_map/all_gather | solution.py:162
  80.9 65.0 %all-gather.13.cloned.1.call-done = bf16[4096,768]{1,0:T(8,128)(2,1)} async-done(((bf16[128,768]{1,0:T(8,128)(2,1)}), bf16[4096,768]{1,0:T(8,128)(2,1)}) %all-gather.13.cloned.1.call-update) | async-done | bytes 6291472 | tf_op jit(solution)/shard_map/all_gather | solution.py:220
  145.9 8.6 copy.74
  154.5 63.0 %all-gather.11.cloned.1.call-done = bf16[4096,768]{1,0:T(8,128)(2,1)} async-done(((bf16[128,768]{1,0:T(8,128)(2,1)}), bf16[4096,768]{1,0:T(8,128)(2,1)}) %all-gather.11.cloned.1.call-update) | async-done | bytes 6291472 | tf_op jit(solution)/shard_map/all_gather | solution.py:219
  217.5 8.7 copy.73
  226.2 50.0 %while.48 = (s32[]{:T(128)}, f32[12,128]{1,0:T(8,128)S(1)}, f32[12,128]{1,0:T(8,128)S(1)}, f32[12,128,64]{1,2,0:T(8,128)}, s32[128]{0:T(128)S(1)}, /*index=5*/s3...) while((s32[]{:T(128)}, f32[12,128]{1,0:T(8,128)S(1)}, ...), condition=%wide.region_5.6_spmd.clone, body=%wide.region_2.5_spmd.clone.sunk | while | flops 210345472 | bytes 21797652 | solution.py:49
  279.2 58.8 %all-gather.17.cloned.1.call-done = bf16[768,3072]{1,0:T(8,128)(2,1)} async-done(((bf16[24,3072]{1,0:T(8,128)(2,1)}), bf16[768,3072]{1,0:T(8,128)(2,1)}) %all-gather.17.cloned.1.call-update) | async-done | bytes 4718608 | tf_op jit(solution)/shard_map/all_gather | solution.py:169
  341.3 61.9 %all-gather.19.cloned.1.call-done = bf16[3072,768]{1,0:T(8,128)(2,1)} async-done(((bf16[96,768]{1,0:T(8,128)(2,1)}), bf16[3072,768]{1,0:T(8,128)(2,1)}) %all-gather.19.cloned.1.call-update) | async-done | bytes 4718608 | tf_op jit(solution)/shard_map/all_gather | solution.py:171
  418.2 5.1 fusion.101
  427.7 43.7 %all_gather.77 = f32[4096,12]{0,1:T(8,128)} all-gather(f32[128,12]{0,1:T(8,128)} %fusion.63), channel_id=1, replica_groups=mesh['head'=2,'blk'=16] {'head','blk'}, dimensions={0}, use_global_device_ids=true | all-gather | bytes 202752 | tf_op jit(solution)/shard_map/all_gather | solution.py:311
  471.4 40.5 %all_gather.75 = f32[4096,12]{0,1:T(8,128)} all-gather(f32[128,12]{0,1:T(8,128)S(1)} %bitcast.205), channel_id=1, replica_groups=mesh['head'=2,'blk'=16] {'head','blk'}, dimensions={0}, use_global_device_ids=true | all-gather | bytes 202752 | tf_op jit(solution)/shard_map/all_gather | solution.py:310
  511.9 75.1 %while.49 = (s32[]{:T(128)}, f32[12,128,64]{1,2,0:T(8,128)}, s32[128]{0:T(128)}, s32[4096]{0:T(1024)}, bf16[4096,768]{0,1:T(8,128)(2,1)}, /*index=5*/bf16[128,12...) while((s32[]{:T(128)}, f32[12,128,64]{1,2,0:T(8,128)}, ...), condition=%wide.region_16.17_spmd.clone, body=%wide.region_15.16_spmd.clone.sunk | while | flops 306970624 | bytes 16298777 | solution.py:49
  588.8 6.7 fusion.72
  596.1 148.0 %while.50 = (s32[]{:T(128)}, f32[128,12,64]{0,2,1:T(8,128)}, f32[128,12,64]{0,2,1:T(8,128)}, bf16[4096,768]{1,0:T(8,128)(2,1)}, s32[4096]{0:T(1024)}, /*index=5*...) while((s32[]{:T(128)}, f32[128,12,64]{0,2,1:T(8,128)}, ...), condition=%wide.region_18.19_spmd.clone, body=%wide.region_17.18_spmd.clone.sunk | while | flops 410976256 | bytes 21215952 | solution.py:49
  628.1 4.7 fusion.185
  664.9 4.8 fusion.185
  683.6 4.8 fusion.185
  720.9 4.7 fusion.185
  747.7 4.8 convolution_bitcast_fusion
  752.5 8.1 copy.85
  763.7 39.6 %all-reduce.18 = (f32[768]{0:T(1024)}, f32[768]{0:T(1024)}, f32[768]{0:T(1024)}, f32[768]{0:T(1024)}, f32[768]{0:T(1024)}, /*index=5*/f32[3072]{0:T(1024)}, f32[768]{0:T(1024)}, f32[768]{0:T(1024)}, f32[768]{0:T(1024)S(1)}) all-reduce(f32[768]{0:T(1024)} %reduce_sum.217, ...), channel_id=3, replica_groups=mesh['head'=2,'blk'=16] {'head','blk'}, use_global_device_ids=true, to_apply=%region_21.22.clone | all-reduce | flops 9216 | bytes 73728
  817.4 115.7 %reduce-scatter.11.cloned.1.call-done = f32[96,768]{1,0:T(8,128)} async-done(((f32[3072,768]{1,0:T(8,128)}), f32[96,768]{1,0:T(8,128)}) %reduce-scatter.11.cloned.1.call-update) | async-done | bytes 294928 | tf_op jit(solution)/shard_map/reduce_scatter | solution.py:344
  933.1 125.2 %reduce-scatter.13.cloned.1.call-done = f32[24,2304]{1,0:T(8,128)} async-done(((f32[768,2304]{1,0:T(8,128)}), f32[24,2304]{1,0:T(8,128)}) %reduce-scatter.13.cloned.1.call-update) | async-done | bytes 221200
  (442 shorter events, 317.2 us)
Async XLA Ops:
  7.2 66.7 %all-gather.9.cloned.1.call-start = ((), (), s32[]{:S(2)}) async-start(), calls=%async_computation.4 | async-start | bytes 3649536 | tf_op jit(solution)/shard_map/all_gather | solution.py:162
  7.9 138.0 %all-gather.13.cloned.1.call-start = ((), (), s32[]{:S(2)}) async-start(), calls=%async_computation.6 | async-start | bytes 6488064 | tf_op jit(solution)/shard_map/all_gather | solution.py:220
  58.0 22.1 %copy-start.28 = (s32[16]{0:T(128)S(1)}, s32[16]{0:T(128)}, u32[]{:S(2)}) copy-start(s32[16]{0:T(128)} %param.23) | copy-start | bytes 196
  77.4 140.1 %all-gather.11.cloned.1.call-start = ((), (), s32[]{:S(2)}) async-start(), calls=%async_computation.5 | async-start | bytes 6488064 | tf_op jit(solution)/shard_map/all_gather | solution.py:219
  78.1 199.1 %all-gather.15.cloned.1.call-start = ((), (), s32[]{:S(2)}) async-start(), calls=%async_computation.7 | async-start | bytes 1216512 | tf_op jit(solution)/shard_map/all_gather | solution.py:165
  78.7 259.3 %all-gather.17.cloned.1.call-start = ((), (), s32[]{:S(2)}) async-start(), calls=%async_computation.8 | async-start | bytes 4866048 | tf_op jit(solution)/shard_map/all_gather | solution.py:169
  79.3 323.8 %all-gather.19.cloned.1.call-start = ((), (), s32[]{:S(2)}) async-start(), calls=%async_computation.9 | async-start | bytes 4866048 | tf_op jit(solution)/shard_map/all_gather | solution.py:171
  79.9 515.6 %all-gather.21.cloned.1.call-start = ((), (), s32[]{:S(2)}) async-start(), calls=%async_computation.10 | async-start | bytes 6488064 | tf_op jit(solution)/shard_map/all_gather | solution.py:314
  80.6 514.9 %all-gather.23.cloned.1.call-start = ((), (), s32[]{:S(2)}) async-start(), calls=%async_computation.11 | async-start | bytes 6488064 | tf_op jit(solution)/shard_map/all_gather | solution.py:315
  276.2 65.0 %copy-start.20 = (s32[4096]{0:T(1024)}, s32[4096]{0:T(1024)S(1)}, u32[]{:S(2)}) copy-start(s32[4096]{0:T(1024)S(1)} %get-tuple-element.1302) | copy-start | bytes 49156
  276.2 65.0 %copy-start.21 = (s32[128]{0:T(128)}, s32[128]{0:T(128)S(1)}, u32[]{:S(2)}) copy-start(s32[128]{0:T(128)S(1)} %get-tuple-element.1304) | copy-start | bytes 1540
  341.2 68.0 %copy-start.3 = (f32[128,3072]{1,0:T(8,128)}, f32[128,3072]{1,0:T(8,128)S(1)}, u32[]{:S(2)}) copy-start(f32[128,3072]{1,0:T(8,128)S(1)} %convolution_add_fusion) | copy-start | bytes 4718596
  341.2 65.7 %copy-start.10 = (bf16[1,128,768]{2,1,0:T(8,128)(2,1)S(1)}, bf16[1,128,768]{2,1,0:T(8,128)(2,1)}, u32[]{:S(2)}) copy-start(bf16[1,128,768]{2,1,0:T(8,128)(2,1)} %param.37) | copy-start | bytes 589828
  403.1 6.1 copy-start.29
  416.2 401.2 %reduce-scatter.7.cloned.1.call-start = ((), (), s32[]{:S(2)}) async-start(), calls=%async_computation.12 | async-start | bytes 2433024 | tf_op jit(solution)/shard_map/reduce_scatter | solution.py:338
  418.2 399.2 %reduce-scatter.9.cloned.1.call-start = ((), (), s32[]{:S(2)}) async-start(), calls=%async_computation.13 | async-start | bytes 9732096 | tf_op jit(solution)/shard_map/reduce_scatter | solution.py:342
  423.4 509.7 %reduce-scatter.11.cloned.1.call-start = ((), (), s32[]{:S(2)}) async-start(), calls=%async_computation.14 | async-start | bytes 9732096 | tf_op jit(solution)/shard_map/reduce_scatter | solution.py:344
  471.4 40.5 %copy-start.24 = (f32[12,128]{1,0:T(8,128)}, f32[12,128]{1,0:T(8,128)S(1)}, u32[]{:S(2)}) copy-start(f32[12,128]{1,0:T(8,128)S(1)} %log_add_fusion) | copy-start | bytes 18436
  521.1 6.0 copy-start.25
  568.3 5.6 copy-start.25
  577.7 5.6 copy-start.25
  595.5 462.9 %reduce-scatter.13.cloned.1.call-start = ((), (), s32[]{:S(2)}) async-start(), calls=%async_computation.15 | async-start | bytes 7299072
  596.1 151.6 %copy-start.9 = (bf16[1,128,768]{2,1,0:T(8,128)(2,1)S(1)}, bf16[1,128,768]{2,1,0:T(8,128)(2,1)}, u32[]{:S(2)}) copy-start(bf16[1,128,768]{2,1,0:T(8,128)(2,1)} %param.22) | copy-start | bytes 589828
  760.6 53.5 %copy-start.2 = (bf16[768,2304]{1,0:T(8,128)(2,1)S(1)}, bf16[768,2304]{1,0:T(8,128)(2,1)}, u32[]{:S(2)}) copy-start(bf16[768,2304]{1,0:T(8,128)(2,1)} %all-gather.9.cloned.1.call-done) | copy-start | bytes 10616836
  (62 other events, 138.0 us)
Sparse Core Ops, SparseCore 0:
  10.9 62.8 all-gather.8
  77.5 68.3 all-gather.12
  149.4 68.0 all-gather.10
  220.2 52.5 all-gather.14
  275.5 62.4 all-gather.16
  340.8 62.3 all-gather.18
  406.0 69.1 all-gather.20
  478.1 67.9 all-gather.22
  552.0 97.5 reduce-scatter.6
  656.9 134.7 reduce-scatter.8
  798.1 134.9 reduce-scatter.10
  940.1 118.1 reduce-scatter.12
where the time goes:
time: 1070 us
  waiting for transfers between devices  508 us (47%)
  local copies, waits for them, and re-layouts  178 us (17%)
  blocking collectives  166 us (16%)
  matrix products  165 us (15%)
  other arithmetic  32.1 us (3%)
  between operations  14.6 us (1%)
    unnamed x13, waiting for transfers between devices  128 us
    reduce_scatter x1, waiting for transfers between devices, per_device(): lax.psum_scatter(grad_w_down, ('head', 'blk'), scatter_dimension=0, tiled...  116 us
    dynamic_slice x64, local copies, waits for them, and re-layouts, loop_body(): lax.dynamic_slice_in_dim(array_item, block_index * block_width, block_wid...  99.5 us
    unnamed x2, blocking collectives  82 us
    all_gather x1, waiting for transfers between devices, per_device(): lax.all_gather(value_flat, ('head', 'blk'), axis=0, tiled=True)  65 us
    all_gather x1, waiting for transfers between devices, per_device(): lax.all_gather(key_flat, ('head', 'blk'), axis=0, tiled=True)  63 us
    all_gather x1, waiting for transfers between devices, per_device(): lax.all_gather(w_down, ('head', 'blk'), axis=0, tiled=True)  61.9 us
    all_gather x1, waiting for transfers between devices, per_device(): lax.all_gather(w_in, ('head', 'blk'), axis=0, tiled=True)  58.8 us
  transfers between devices with their start and end apart: 12, of which 7 were waited for; matrix products, arithmetic and copies ran while one was open for 33% of the time, Pallas kernels for 0%

commit v1 on v0

v1 whole, which is shorter than its diff:
```python
from functools import partial

import jax
import jax.numpy as jnp
from jax import lax
from jax.experimental import pallas as pl
from jax.experimental.pallas import tpu as pltpu
from jax.sharding import PartitionSpec as P

HEADS = 12
HEAD_DIM = 64
Z, Y, C = 4, 2, 2
GROUP = HEADS // Z
QW = GROUP * HEAD_DIM
KVW = 2 * QW
LANE = 128
WPAD = 768
VEC_AT = 640
masked_score = -1e30
norm_epsilon = 1e-06
BF = jnp.bfloat16
F32 = jnp.float32
AXES = ("head", "blk")


def dot(a, b, ca=1, cb=0):
    return lax.dot_general(a, b, (((ca,), (cb,)), ((), ())), preferred_element_type=F32)


def place_keys(pos_ref, src_refs, kvs, sems, zo):
    x, z, y, c = pos_ref[0], pos_ref[1], pos_ref[2], pos_ref[3]
    copies = []
    for dc in range(2):
        for dxy in range(4):
            for o in range(zo):
                for k in range(Z):
                    xx = lax.rem(x + dxy // 2, 2)
                    yy = lax.rem(y + dxy % 2, 2)
                    cc = lax.rem(c + dc, 2)
                    zz = lax.rem(z + k, Z)
                    at = (((o * Z + zz) * Y + yy) * C + cc) * 2 + xx
                    copies.append(
                        pltpu.make_async_copy(
                            src_refs[dc].at[dxy, o, k], kvs.at[at], sems.at[len(copies)]
                        )
                    )
    for copy in copies:
        copy.start()
    return copies


def head_mask_rows(block, offset):
    lanes = lax.broadcasted_iota(jnp.int32, block.shape, 1) // HEAD_DIM
    parts = []
    for h in range(GROUP):
        parts.append(jnp.where(lanes == offset[h], block, jnp.zeros_like(block)))
    return jnp.concatenate(parts, axis=0)


def widen_q(q):
    return jnp.concatenate([q, jnp.zeros((q.shape[0], HEAD_DIM), q.dtype)], axis=1)


def widen_v(v):
    return jnp.concatenate(
        [
            jnp.zeros((v.shape[0], HEAD_DIM), v.dtype),
            v[:, 2 * HEAD_DIM :],
            v[:, : 2 * HEAD_DIM],
        ],
        axis=1,
    )


V_ROW = (2, 3, 1)


def allowed_keys(rng_ref, i, first, rows):
    kid = first + lax.broadcasted_iota(jnp.int32, (rows, LANE), 0)
    ok = (kid >= rng_ref[i, 0:1, :]) & (kid < rng_ref[i, 1:2, :])
    return jnp.concatenate([ok] * GROUP, axis=1)


def attention_forward(
    zo, tile, pos_ref, lim_ref, q_ref, rng_ref, kva_ref, kvb_ref, o_ref, ob_ref, lse_ref,
    kvs, qm, m_s, l_s, acc, sems,
):
    copies = place_keys(pos_ref, (kva_ref, kvb_ref), kvs, sems, zo)
    for i in range(Z):
        qm[i] = head_mask_rows(widen_q(q_ref[i]), (0, 1, 2))
    m_s[...] = jnp.full(m_s.shape, masked_score, F32)
    l_s[...] = jnp.zeros(l_s.shape, F32)
    acc[...] = jnp.zeros(acc.shape, F32)
    for copy in copies:
        copy.wait()
    chunks = tile // LANE

    def step(i, j, masked):
        kt = kvs[pl.ds(j * chunks, chunks)].reshape(tile, KVW)
        s = dot(kt[:, :256], qm[i], 1, 1)
        if masked:
            ok = allowed_keys(rng_ref, i, j * tile, tile)
            s = jnp.where(ok, s, masked_score)
        m_old = m_s[i]
        m_new = jnp.maximum(m_old, jnp.max(s, axis=0, keepdims=True))
        p = jnp.exp(s - m_new)
        if masked:
            p = jnp.where(ok, p, 0.0)
        f = jnp.exp(m_old - m_new)
        l_s[i] = l_s[i] * f + jnp.sum(p, axis=0, keepdims=True)
        m_s[i] = m_new
        pv = dot(kt[:, 128:], p.astype(BF), 0, 0)
        for h in range(GROUP):
            r = V_ROW[h] * HEAD_DIM
            acc[i, h] = (
                acc[i, h] * f[:, h * LANE : (h + 1) * LANE]
                + pv[r : r + HEAD_DIM, h * LANE : (h + 1) * LANE]
            )

    def body(j, carry):
        lo, hi = j * tile, (j + 1) * tile
        for i in range(Z):
            live = (lim_ref[i, 1] > lo) & (lim_ref[i, 0] < hi)
            inside = (lim_ref[i, 2] <= lo) & (lim_ref[i, 3] >= hi)
            pl.when(live & inside)(partial(step, i, j, False))
            pl.when(live & jnp.logical_not(inside))(partial(step, i, j, True))
        return carry

    lax.fori_loop(0, kvs.shape[0] // chunks, body, 0)
    for i in range(Z):
        l = l_s[i]
        lse_ref[i] = m_s[i] + jnp.log(l)
        parts = []
        for h in range(GROUP):
            parts.append((acc[i, h] / l[:, h * LANE : (h + 1) * LANE]).T)
        o = jnp.concatenate(parts, axis=1)
        o_ref[i] = o
        ob_ref[i] = o.astype(BF)


def attention_backward(
    zo, tile, pos_ref, lim_ref, q_ref, do_ref, o_ref, lse_ref, rng_ref, kva_ref, kvb_ref,
    dq_ref, dkv_ref, kvs, qm, dom, delta_s, dqt, dk_s, dv_s, sems,
):
    copies = place_keys(pos_ref, (kva_ref, kvb_ref), kvs, sems, zo)
    for i in range(Z):
        qm[i] = head_mask_rows(widen_q(q_ref[i]), (0, 1, 2))
        dom[i] = head_mask_rows(widen_v(do_ref[i]), V_ROW)
        prod = (do_ref[i].astype(F32) * o_ref[i]).T
        rows = []
        for h in range(GROUP):
            rows.append(
                jnp.sum(prod[h * HEAD_DIM : (h + 1) * HEAD_DIM], axis=0, keepdims=True)
            )
        delta_s[i] = jnp.concatenate(rows, axis=1)
    dqt[...] = jnp.zeros(dqt.shape, F32)
    for copy in copies:
        copy.wait()
    chunks = tile // LANE

    def step(i, j, masked):
        kt = kvs[pl.ds(j * chunks, chunks)].reshape(tile, KVW)
        s = dot(kt[:, :256], qm[i], 1, 1)
        p = jnp.exp(s - lse_ref[i])
        if masked:
            ok = allowed_keys(rng_ref, i, j * tile, tile)
            p = jnp.where(ok, p, 0.0)
        dp = dot(kt[:, 128:], dom[i], 1, 1)
        ds = (p * (dp - delta_s[i])).astype(BF)
        dv_s[...] += dot(p.astype(BF), dom[i], 1, 0)
        dk_s[...] += dot(ds, qm[i], 1, 0)
        dq = dot(kt[:, :256], ds, 0, 0)
        for h in range(GROUP):
            dqt[i, h] += dq[h * HEAD_DIM : (h + 1) * HEAD_DIM, h * LANE : (h + 1) * LANE]

    def body(j, carry):
        lo, hi = j * tile, (j + 1) * tile
        dk_s[...] = jnp.zeros(dk_s.shape, F32)
        dv_s[...] = jnp.zeros(dv_s.shape, F32)
        for i in range(Z):
            live = (lim_ref[i, 1] > lo) & (lim_ref[i, 0] < hi)
            inside = (lim_ref[i, 2] <= lo) & (lim_ref[i, 3] >= hi)
            pl.when(live & inside)(partial(step, i, j, False))
            pl.when(live & jnp.logical_not(inside))(partial(step, i, j, True))
        dk, dv = dk_s[...], dv_s[...]
        out = jnp.concatenate([dk[:, :128], dk[:, 128:] + dv[:, :128], dv[:, 128:]], axis=1)
        dkv_ref[pl.ds(j * chunks, chunks)] = out.astype(BF).reshape(chunks, LANE, KVW)
        return carry

    lax.fori_loop(0, kvs.shape[0] // chunks, body, 0)
    for i in range(Z):
        parts = []
        for h in range(GROUP):
            parts.append((dqt[i, h] * (HEAD_DIM**-0.5)).T)
        dq_ref[i] = jnp.concatenate(parts, axis=1).astype(BF)


def vmem():
    return pl.BlockSpec(memory_space=pltpu.VMEM)


def smem():
    return pl.BlockSpec(memory_space=pltpu.SMEM)


def hbm():
    return pl.BlockSpec(memory_space=pl.ANY)


def run_forward(pos, lim, q, rng, kva, kvb, zo):
    tile = 512
    nc = 32 * zo
    return pl.pallas_call(
        partial(attention_forward, zo, tile),
        out_shape=(
            jax.ShapeDtypeStruct((Z, LANE, QW), F32),
            jax.ShapeDtypeStruct((Z, LANE, QW), BF),
            jax.ShapeDtypeStruct((Z, 1, GROUP * LANE), F32),
        ),
        in_specs=[smem(), smem(), vmem(), vmem(), hbm(), hbm()],
        out_specs=(vmem(), vmem(), vmem()),
        scratch_shapes=[
            pltpu.VMEM((nc, LANE, KVW), BF),
            pltpu.VMEM((Z, GROUP * LANE, 256), BF),
            pltpu.VMEM((Z, 1, GROUP * LANE), F32),
            pltpu.VMEM((Z, 1, GROUP * LANE), F32),
            pltpu.VMEM((Z, GROUP, HEAD_DIM, LANE), F32),
            pltpu.SemaphoreType.DMA((8 * zo * Z,)),
        ],
        compiler_params=pltpu.CompilerParams(vmem_limit_bytes=(16 + 4 * zo) << 20),
    )(pos, lim, q, rng, kva, kvb)


def run_backward(pos, lim, q, do, o, lse, rng, kva, kvb, zo):
    tile = 512
    nc = 32 * zo
    return pl.pallas_call(
        partial(attention_backward, zo, tile),
        out_shape=(
            jax.ShapeDtypeStruct((Z, LANE, QW), BF),
            jax.ShapeDtypeStruct((nc, LANE, KVW), BF),
        ),
        in_specs=[smem(), smem(), vmem(), vmem(), vmem(), vmem(), vmem(), hbm(), hbm()],
        out_specs=(vmem(), vmem()),
        scratch_shapes=[
            pltpu.VMEM((nc, LANE, KVW), BF),
            pltpu.VMEM((Z, GROUP * LANE, 256), BF),
            pltpu.VMEM((Z, GROUP * LANE, 256), BF),
            pltpu.VMEM((Z, 1, GROUP * LANE), F32),
            pltpu.VMEM((Z, GROUP, HEAD_DIM, LANE), F32),
            pltpu.VMEM((tile, 256), F32),
            pltpu.VMEM((tile, 256), F32),
            pltpu.SemaphoreType.DMA((8 * zo * Z,)),
        ],
        compiler_params=pltpu.CompilerParams(vmem_limit_bytes=(18 + 7 * zo) << 20),
    )(pos, lim, q, do, o, lse, rng, kva, kvb)


def normalize(values):
    centered = values - jnp.mean(values, axis=1, keepdims=True)
    inverse_root = lax.rsqrt(jnp.mean(centered * centered, axis=1, keepdims=True) + norm_epsilon)
    return (centered * inverse_root, inverse_root)


def normalize_back(grad_norm, normed, inverse_root):
    return inverse_root * (
        grad_norm
        - jnp.mean(grad_norm, axis=1, keepdims=True)
        - normed * jnp.mean(grad_norm * normed, axis=1, keepdims=True)
    )


class Place:
    def __init__(self, nb):
        self.nb = nb
        self.zo = nb // (Z * Y * C)
        self.x = lax.axis_index("head")
        b = lax.axis_index("blk")
        self.c = b % 2
        self.y = b // 2 % 2
        self.z = b // 4 % 4
        self.o = b // 16

    def move(self, a, dx=0, do=0, dz=0, dy=0, dc=0):
        pairs = []
        for x in range(2):
            for o in range(self.zo):
                for z in range(Z):
                    for y in range(Y):
                        for c in range(C):
                            src = (
                                (x + dx) % 2,
                                (o + do) % self.zo,
                                (z + dz) % Z,
                                (y + dy) % Y,
                                (c + dc) % C,
                            )
                            pairs.append((self.lin(*src), self.lin(x, o, z, y, c)))
        return lax.ppermute(a, AXES, pairs)

    def lin(self, x, o, z, y, c):
        return x * self.nb + ((o * Z + z) * Y + y) * C + c

    def trade_z(self, pieces):
        return [pieces[0]] + [self.move(pieces[Z - m], dz=m) for m in range(1, Z)]

    def gather_o(self, a):
        if self.zo == 1:
            return a[None]
        got = jnp.stack([a] + [self.move(a, do=k) for k in range(1, self.zo)])
        return jnp.roll(got, self.o, axis=0)

    def scatter_o(self, a):
        if self.zo == 1:
            return a[0]
        mine = jnp.roll(a, -self.o, axis=0)
        total = mine[0].astype(F32)
        for k in range(1, self.zo):
            total = total + self.move(mine[self.zo - k], do=k).astype(F32)
        return total.astype(a.dtype)


def pick(a, index, axis):
    return lax.dynamic_index_in_dim(a, index, axis, keepdims=False)


def per_device(
    nb,
    tokens,
    doc_starts,
    w_qkv,
    b_query,
    b_value,
    w_out,
    b_out,
    gain_attn,
    shift_attn,
    w_in,
    b_in,
    w_down,
    b_down,
    gain_ffn,
    shift_ffn,
    cotangent,
):
    at = Place(nb)
    zo, x, y, z, c = at.zo, at.x, at.y, at.z, at.c
    inputs = tokens[0]
    rows, D = inputs.shape
    FF = w_in.shape[1]
    S = D // (32)
    R = S // zo
    FS = FF // 32
    FR = FS // zo
    FC = FF // 2
    total_tokens = rows * 2 * nb

    def slab(a):
        g = at.gather_o(a)
        return g.reshape((g.shape[0] * g.shape[1],) + g.shape[2:])

    small = [b_query, b_value, b_out, gain_attn, shift_attn, b_down, gain_ffn, shift_ffn]
    vec_cols = jnp.concatenate(
        [slab(v)[:, None] for v in small] + [slab(b_in).reshape(4, S).T], axis=1
    )
    vec_cols = jnp.pad(vec_cols, ((0, 0), (0, LANE - vec_cols.shape[1])))
    wq = slab(w_qkv).reshape(S, 3, Z, GROUP, HEAD_DIM)
    order = [(1, 0), (1, 1), (1, 2), (2, 2), (2, 0), (2, 1), (0, 0), (0, 1), (0, 2)]
    w4 = jnp.stack([wq[:, a, :, h] for a, h in order], axis=2)
    w4 = w4.transpose(1, 0, 2, 3).reshape(Z, S, 3 * QW)
    w4 = jnp.concatenate(
        [
            w4,
            jnp.zeros((Z, S, VEC_AT - 3 * QW), BF),
            jnp.broadcast_to(vec_cols[None], (Z, S, LANE)),
        ],
        axis=2,
    )
    w4 = jnp.roll(w4, -z, axis=0)
    got = at.trade_z([jnp.concatenate([inputs, w4[m]], axis=0) for m in range(Z)])
    xcol = jnp.concatenate([g[:rows] for g in got], axis=0)
    wz = jnp.roll(jnp.stack([g[rows:] for g in got]), z, axis=0)
    wp = jnp.stack([wz, at.move(wz, dy=1), at.move(wz, dx=1), at.move(wz, dx=1, dy=1)])
    wc = jnp.stack([wp, at.move(wp, dc=1)]).reshape(2, 2, 2, Z, S, WPAD)
    wc = jnp.roll(wc, (c, x, y), axis=(0, 1, 2))
    wfull = wc.reshape(2, 2, 2, Z, zo, R, WPAD).transpose(1, 4, 3, 2, 0, 5, 6).reshape(D, WPAD)
    w_z = wfull[:, : 3 * QW]
    vecs = wfull[:, VEC_AT:].astype(F32).T
    bq = lax.dynamic_slice_in_dim(vecs[0], z * QW, QW, 0)
    bv = lax.dynamic_slice_in_dim(vecs[1], z * QW, QW, 0)
    bias = jnp.concatenate([jnp.zeros((QW,), F32), bv[2 * HEAD_DIM :], bv[: 2 * HEAD_DIM], bq])
    f_bout, f_g1, f_s1, f_bdown, f_g2, f_s2 = [vecs[j] for j in range(2, 8)]
    vslab = wc[..., VEC_AT + 8 : VEC_AT + 12]
    f_bin = pick(vslab, c, 0).transpose(0, 2, 1, 4, 3).reshape(FC).astype(F32)

    projected = (dot(xcol, w_z) + bias[None]).astype(BF)
    kv = projected[:, :KVW].reshape(Z, rows, KVW)
    q = projected[:, KVW:].reshape(Z, rows, QW) * jnp.asarray(HEAD_DIM**-0.5, BF)

    kvo = at.gather_o(kv)
    kva = jnp.stack([kvo, at.move(kvo, dy=1), at.move(kvo, dx=1), at.move(kvo, dx=1, dy=1)])
    kvb = at.move(kva, dc=1)

    zk = (z + jnp.arange(Z)) % Z
    first = ((((at.o * Z + zk) * Y + y) * C + c) * 2 + x) * rows
    tok = first[:, None] + jnp.arange(rows)[None]
    ends = jnp.concatenate([doc_starts[1:], jnp.full((1,), total_tokens, jnp.int32)])
    begun = tok[:, :, None] >= doc_starts[None, None, :]
    start_t = jnp.max(jnp.where(begun, doc_starts[None, None, :], 0), axis=2)
    end_t = jnp.min(jnp.where(ends[None, None, :] > tok[:, :, None], ends[None, None, :], total_tokens), axis=2)
    rng = jnp.stack([start_t, end_t], axis=1)
    lim = jnp.stack([start_t[:, 0], end_t[:, -1], start_t[:, -1], end_t[:, 0]], axis=1)
    pos = jnp.stack([x, z, y, c]).astype(jnp.int32)

    o_att, ob_att, lse = run_forward(pos, lim, q, rng, kva, kvb, zo)

    wi = slab(w_in).reshape(S, 2, zo, Z, Y, C, FR).transpose(5, 0, 1, 3, 4, 2, 6).reshape(2, S, FC)
    wi_other = at.move(pick(wi, 1 - c, 0), dc=1)
    a_piece = jnp.roll(jnp.stack([pick(wi, c, 0), wi_other]), c, axis=0)
    b_piece = jnp.concatenate([slab(w_down), slab(w_out)], axis=0)

    def gather_chips(piece, x_first):
        zp = jnp.stack([piece] + [at.move(piece, dz=k) for k in range(1, Z)])
        zp = jnp.roll(zp, z, axis=0)
        if x_first:
            p1 = jnp.roll(jnp.stack([zp, at.move(zp, dx=1)]), x, axis=0)
            p2 = jnp.roll(jnp.stack([p1, at.move(p1, dy=1)]), y, axis=0)
            return jnp.moveaxis(p2, 0, 2)
        p1 = jnp.roll(jnp.stack([zp, at.move(zp, dy=1)]), y, axis=0)
        p2 = jnp.roll(jnp.stack([p1, at.move(p1, dx=1)]), x, axis=0)
        return jnp.moveaxis(p2, 1, 2)

    wa = gather_chips(a_piece, True)
    wb = gather_chips(b_piece, False)
    win_c = wa.reshape(2, Z, Y, C, zo, R, FC).transpose(0, 4, 1, 2, 3, 5, 6).reshape(D, FC)
    wdn_c = wb[:, :, :, :FS].reshape(FC, D)
    wo = wb[:, :, :, FS:]
    wo = jnp.roll(jnp.stack([wo, at.move(wo, dc=1)]), c, axis=0)
    wo = wo.reshape(C, 2, Z, Y, zo, R, D).transpose(1, 4, 2, 3, 0, 5, 6).reshape(D, D)

    ob = jnp.stack(at.trade_z([ob_att[k] for k in range(Z)]))
    ob = jnp.roll(ob, z, axis=0).transpose(1, 0, 2).reshape(rows, D)
    r1 = dot(ob, wo) + f_bout[None] + inputs.astype(F32)
    n1, rs1 = normalize(r1)
    h1 = n1 * f_g1[None] + f_s1[None]
    h1b = h1.astype(BF)

    def both(a):
        return jnp.roll(jnp.stack([a, at.move(a, dc=1)]), c, axis=0).reshape(2 * rows, -1)

    def split_sum(part):
        p = part.reshape(2, rows, -1)
        return pick(p, c, 0) + at.move(pick(p, 1 - c, 0), dc=1)

    hb = both(h1b)
    u = dot(hb, win_c) + f_bin[None]
    g, gelu_back = jax.vjp(partial(jax.nn.gelu, approximate=True), u)
    gb = g.astype(BF)
    r2 = split_sum(dot(gb, wdn_c)) + f_bdown[None] + h1
    n2, rs2 = normalize(r2)
    layer_out = (n2 * f_g2[None] + f_s2[None]).astype(BF)
    cot = cotangent[0].astype(F32)
    g_gain2 = jnp.sum(cot * n2, axis=0)
    g_shift2 = jnp.sum(cot, axis=0)
    dr2 = normalize_back(cot * f_g2[None], n2, rs2)
    g_bdown = jnp.sum(dr2, axis=0)
    dfb = both(dr2.astype(BF))
    dub = gelu_back(dot(dfb, wdn_c, 1, 1))[0].astype(BF)
    g_bin = jnp.sum(dub.astype(F32), axis=0)
    dh1 = split_sum(dot(dub, win_c, 1, 1)) + dr2
    g_gain1 = jnp.sum(dh1 * n1, axis=0)
    g_shift1 = jnp.sum(dh1, axis=0)
    dr1 = normalize_back(dh1 * f_g1[None], n1, rs1)
    g_bout = jnp.sum(dr1, axis=0)
    dab = dr1.astype(BF)
    dob = dot(dab, wo, 1, 1).astype(BF)
    dobs = jnp.roll(dob.reshape(rows, Z, QW).transpose(1, 0, 2), -z, axis=0)
    do_att = jnp.stack(at.trade_z([dobs[m] for m in range(Z)]))

    dq, dkv = run_backward(pos, lim, q, do_att, o_att, lse, rng, kva, kvb, zo)

    gw_in = dot(hb, dub, 0, 0).astype(BF)
    gw_dn = dot(gb, dfb, 0, 0).astype(BF)
    gw_out = dot(ob, dab, 0, 0)
    ga = gw_in.reshape(2, zo, Z, Y, C, R, FC).transpose(0, 2, 3, 4, 1, 5, 6).reshape(2, Z, Y, C * S, FC)
    go = gw_out.reshape(2, zo, Z, Y, C, R, D).transpose(4, 0, 2, 3, 1, 5, 6).reshape(C, 2, Z, Y, S, D)
    go = (pick(go, c, 0) + at.move(pick(go, 1 - c, 0).astype(BF), dc=1).astype(F32)).astype(BF)
    gb_all = jnp.concatenate([gw_dn.reshape(2, Z, Y, FS, D), go], axis=3)

    def fold(a, axis, index, **kw):
        return (
            pick(a, index, axis).astype(F32)
            + at.move(pick(a, 1 - index, axis), **kw).astype(F32)
        ).astype(BF)

    def sum_z(a):
        a = jnp.roll(a, -z, axis=0)
        return sum(p.astype(F32) for p in at.trade_z([a[m] for m in range(Z)]))

    ga = fold(fold(ga, 0, x, dx=1), 1, y, dy=1)
    ga = sum_z(ga).reshape(C, S, FC)
    gbs = fold(fold(gb_all, 2, y, dy=1), 0, x, dx=1)
    gbs = sum_z(gbs)
    g_wdn = at.scatter_o(gbs[:FS].reshape(zo, FR, D))
    g_wout = at.scatter_o(gbs[FS:].reshape(zo, R, D))
    ga_own = pick(ga, c, 0)
    ga_oth = at.move(pick(ga, 1 - c, 0).astype(BF), dc=1).astype(F32)
    g_win = jnp.roll(jnp.stack([ga_own, ga_oth]), c, axis=0)
    g_win = g_win.reshape(C, S, 2, Z, Y, zo, FR).transpose(1, 2, 5, 3, 4, 0, 6).reshape(S, FF)
    g_win = at.scatter_o(g_win.reshape(zo, R, FF))

    dkv = at.scatter_o(dkv.reshape(zo, Z, Y, C, 2, rows, KVW))
    dkv = fold(dkv, 2, c, dc=1)
    dkv = jnp.roll(dkv, (-y, -x), axis=(1, 2))
    dkv = (
        dkv[:, 0, 0].astype(F32)
        + at.move(dkv[:, 1, 0], dy=1).astype(F32)
        + at.move(dkv[:, 0, 1], dx=1).astype(F32)
        + at.move(dkv[:, 1, 1], dx=1, dy=1).astype(F32)
    )
    dkv = jnp.roll(dkv, -z, axis=0).astype(BF).reshape(Z * rows, KVW)
    dqkv = jnp.concatenate([dkv, dq.reshape(Z * rows, QW)], axis=1)

    dxp = dot(dqkv, w_z, 1, 1).reshape(Z, rows, D)
    dxs = at.trade_z([dxp[0]] + [dxp[m].astype(BF) for m in range(1, Z)])
    grad_inputs = dr1 + sum(p.astype(F32) for p in dxs)

    gw = dot(xcol, dqkv, 0, 0)
    colsum = jnp.sum(dqkv.astype(F32), axis=0)
    g_bq = lax.dynamic_update_slice(jnp.zeros((D,), F32), colsum[KVW:], (z * QW,))
    sv = colsum[QW:KVW]
    sv = jnp.concatenate([sv[HEAD_DIM:], sv[:HEAD_DIM]])
    g_bv = lax.dynamic_update_slice(jnp.zeros((D,), F32), sv, (z * QW,))
    vrows = jnp.stack([g_bq, g_bv, g_bout, g_gain1, g_shift1, g_bdown, g_gain2, g_shift2])

    def by_slab(a):
        a = a.reshape(2, zo, Z, Y, C, R, -1).transpose(4, 0, 3, 2, 1, 5, 6)
        return a.reshape(C, 2, Y, Z, S, -1)

    gbin = g_bin.reshape(2, Z, Y, 4, S).transpose(0, 2, 1, 4, 3)
    gbin = jnp.stack([gbin, jnp.zeros_like(gbin)])
    gbin = jnp.roll(gbin, c, axis=0)
    gq = jnp.concatenate(
        [
            by_slab(gw),
            jnp.zeros((C, 2, Y, Z, S, VEC_AT - 3 * QW), F32),
            by_slab(vrows.T),
            gbin,
            jnp.zeros((C, 2, Y, Z, S, LANE - 12), F32),
        ],
        axis=5,
    ).astype(BF)
    gq = fold(gq, 0, c, dc=1)
    gq = jnp.roll(gq, (-x, -y), axis=(0, 1))
    gq = (
        gq[0, 0].astype(F32)
        + at.move(gq[0, 1], dy=1).astype(F32)
        + at.move(gq[1, 0], dx=1).astype(F32)
        + at.move(gq[1, 1], dx=1, dy=1).astype(F32)
    ).astype(BF)
    gq = jnp.roll(gq, -z, axis=0)
    gq = jnp.roll(jnp.stack(at.trade_z([gq[m] for m in range(Z)])), z, axis=0).astype(F32)
    gwq = gq[:, :, : 3 * QW].reshape(Z, S, 9, HEAD_DIM)
    inv = [order.index((a, h)) for a in range(3) for h in range(GROUP)]
    gwq = jnp.stack([gwq[:, :, i] for i in inv], axis=2).reshape(Z, S, 3, QW)
    gwq = gwq.transpose(1, 2, 0, 3).reshape(S, 3 * D)
    g_wqkv = at.scatter_o(gwq.reshape(zo, R, 3 * D))
    gv = jnp.sum(gq[:, :, VEC_AT:], axis=0)
    outs = [at.scatter_o(gv[:, j].reshape(zo, R)) for j in range(8)]
    g_b_in = at.scatter_o(gv[:, 8:12].T.reshape(zo, FR))
    return (
        layer_out[None],
        grad_inputs[None],
        g_wqkv,
        outs[0],
        outs[1],
        g_wout,
        outs[2],
        outs[3],
        outs[4],
        g_win,
        g_b_in,
        g_wdn,
        outs[5],
        outs[6],
        outs[7],
    )


def solution(mesh):
    nb = mesh.shape["blk"]
    w2 = P(("head", "blk"), None)
    w1 = P(("head", "blk"))
    tok = P("blk", "head", None)
    return jax.shard_map(
        partial(per_device, nb),
        mesh=mesh,
        in_specs=(tok, P(), w2, w1, w1, w2, w1, w1, w1, w2, w1, w2, w1, w1, w1, tok),
        out_specs=(tok, tok, w2, w1, w1, w2, w1, w1, w1, w2, w1, w2, w1, w1, w1),
        check_vma=False,
    )
```

time: 1070 us -> 402 us (0.38)
  waiting for transfers between devices: 508 us -> 138 us
  blocking collectives: 166 us -> 0 us
  matrix products: 165 us -> 18.8 us
  local copies, waits for them, and re-layouts: 178 us -> 50.1 us
  starting transfers between devices: 0.66 us -> 103 us
  Pallas kernels: 0 us -> 36 us
  other arithmetic: 32.1 us -> 48.6 us
  between operations: 14.6 us -> 2.86 us
    all_gather x8 -> x0, waiting for transfers between devices: 265 us -> none  [the longest x1 65 us: per_device(): lax.all_gather(value_flat, ('head', 'blk'), axis=0, tiled=True)]
    dot_general x68 -> x12, matrix products: 165 us -> 18.8 us  [dot(): lax.dot_general(a, b, (((ca,), (cb,)), ((), ())), preferred_element_type=...]
    ppermute x0 -> x59, waiting for transfers between devices: none -> 138 us  [move(): return lax.ppermute(a, AXES, pairs)]
    unnamed x13 -> x0, waiting for transfers between devices: 128 us -> none
    reduce_scatter x3 -> x0, waiting for transfers between devices: 116 us -> none  [the longest x1 116 us: per_device(): lax.psum_scatter(grad_w_down, ('head', 'blk'), scatter_dimension=0, tiled...]
    ppermute x0 -> x59, starting transfers between devices: none -> 103 us  [move(): return lax.ppermute(a, AXES, pairs)]
    dynamic_slice x64 -> x5, local copies, waits for them, and re-layouts: 99.5 us -> 2.07 us  [the longest x1 1.19 us: per_device(): wo = jnp.roll(jnp.stack([wo, at.move(wo, dc=1)]), c, axis=0)]
    all_gather x2 -> x0, blocking collectives: 84.2 us -> none  [the longest x1 43.7 us: per_device(): lax.all_gather(row_delta.T, ('head', 'blk'), axis=0, tiled=True)]
  transfers between devices with their start and end apart: 12 -> 59, of which waited for: 7 -> 21; matrix products, arithmetic and copies ran while one was open for 33% -> 23% of each run, Pallas kernels for 0% -> 9%
where the time goes in v1:
time: 402 us; the launch traced here: 398 us
  waiting for transfers between devices  138 us (34%)
  starting transfers between devices  103 us (26%)
  local copies, waits for them, and re-layouts  50.1 us (12%)
  other arithmetic  48.6 us (12%)
  Pallas kernels  36 us (9%)
  matrix products  18.8 us (5%)
    ppermute x59, waiting for transfers between devices, move(): return lax.ppermute(a, AXES, pairs)  138 us
    ppermute x59, starting transfers between devices, move(): return lax.ppermute(a, AXES, pairs)  103 us
    pallas_call x1, Pallas kernels, run_backward(): pl.pallas_call(partial(attention_backward, zo, tile), out_shape=(jax.Shap...  19.1 us
    dot_general x12, matrix products, dot(): lax.dot_general(a, b, (((ca,), (cb,)), ((), ())), preferred_element_type=...  18.8 us
    pallas_call x1, Pallas kernels, run_forward(): pl.pallas_call(partial(attention_forward, zo, tile), out_shape=(jax.Shape...  16.9 us
  transfers between devices with their start and end apart: 59, of which 21 were waited for; matrix products, arithmetic and copies ran while one was open for 23% of the time, Pallas kernels for 9%

profile of v1, /device:TPU:0, one launch (start us, length us, event | category | flops | bytes accessed | tf_op | source)
XLA Modules:
  0.0 397.7 jit_solution(6785847052519676413)
XLA Ops:
  22.0 19.6 %collective-permute-start.22 = (bf16[2,24,1536]{2,1,0:T(8,128)(2,1)S(1)}, bf16[2,24,1536]{2,1,0:T(8,128)(2,1)S(1)}, u32[]{:S(2)}, u32[]{:S(2)}) collective-permute-start(bf16[2,24,1536]{2,1,0:T(8,128)(2,1)S(1)} %get-tuple-element.62), channel_id=1, source_target_pairs={{4,0},{5,1},{6,2},{7,3},{8,4},{9,5},{10,6},{11,7},{12,8},{13,9},{1... | collective-permute-start | bytes 442376 | tf_op jit(solution)/shard_map/ppermute | solution.py:299
  45.3 12.2 %collective-permute-start.24 = (bf16[2,24,1536]{2,1,0:T(8,128)(2,1)S(1)}, bf16[2,24,1536]{2,1,0:T(8,128)(2,1)S(1)}, u32[]{:S(2)}, u32[]{:S(2)}) collective-permute-start(bf16[2,24,1536]{2,1,0:T(8,128)(2,1)S(1)} %get-tuple-element.62), channel_id=1, source_target_pairs={{12,0},{13,1},{14,2},{15,3},{0,4},{1,5},{2,6},{3,7},{4,8},{5,9},{6... | collective-permute-start | bytes 442376 | tf_op jit(solution)/shard_map/ppermute | solution.py:299
  68.9 11.2 %collective-permute-done.4 = bf16[4,24,768]{2,1,0:T(8,128)(2,1)S(1)} collective-permute-done((bf16[4,24,768]{2,1,0:T(8,128)(2,1)S(1)}, bf16[4,24,768]{2,1,0:T(8,128)(2,1)S(1)}, u32[]{:S(2)}, u32[]{:S(2)}) %collective-permute-start.4) | collective-permute-done | bytes 147488 | tf_op jit(solution)/shard_map/ppermute | solution.py:299
  103.2 30.7 %collective-permute-done.9 = bf16[1,4,128,384]{3,2,1,0:T(8,128)(2,1)S(1)} collective-permute-done((bf16[1,4,128,384]{3,2,1,0:T(8,128)(2,1)S(1)}, bf16[1,4,128,384]{3,2,1,0:T(8,128)(2,1)S(1)}, u32[]{:S(2)}, u32[]{:S(2)}) %collective-permute-start.9) | collective-permute-done | bytes 393248 | tf_op jit(solution)/shard_map/ppermute | solution.py:299
  133.9 5.3 %collective-permute-done.8 = bf16[1,4,128,384]{3,2,1,0:T(8,128)(2,1)S(1)} collective-permute-done((bf16[1,4,128,384]{3,2,1,0:T(8,128)(2,1)S(1)}, bf16[1,4,128,384]{3,2,1,0:T(8,128)(2,1)S(1)}, u32[]{:S(2)}, u32[]{:S(2)}) %collective-permute-start.8) | collective-permute-done | bytes 393248 | tf_op jit(solution)/shard_map/ppermute | solution.py:299
  144.0 4.6 %fusion.4 = bf16[2,4,2,120,768]{4,3,1,2,0:T(8,128)(2,1)S(1)} fusion(s32[]{:T(128)S(6)} %select_n.272, bf16[1,2,4,120,768]{4,3,2,1,0:T(8,128)(2,1)} %fusion.187, bf16[1,2,4,120,768]{4,3,2,1,0:T(8,128)(2,1)} %bitcast.63), kind=kLoop, calls=%fused_computation.21 | loop fusion | flops 4423680 | bytes 5898244 | tf_op jit(solution)/shard_map/transpose | solution.py:431
  149.9 4.7 %fusion.8 = bf16[2,2,4,2,24,1536]{5,4,3,0,2,1:T(8,128)(2,1)} fusion(s32[]{:T(128)S(6)} %select_n.274, bf16[1,2,4,2,24,1536]{5,4,3,0,2,1:T(8,128)(2,1)S(1)} %copy-done.18, bf16[1,2,4,2,24,1536]{5,4,3,0,2,1:T(8,128)(2,1)} %bitcast.83), kind=kLoop, calls=%fused_computation.33 | loop fusion | flops 3538944 | bytes 4718596 | tf_op jit(solution)/shard_map/jit(_roll_dynamic)/concatenate | solution.py:427
  156.4 16.9 %shard_map.271 = (f32[4,128,192]{2,1,0:T(8,128)S(1)}, bf16[4,128,192]{2,1,0:T(8,128)(2,1)S(1)}, f32[4,1,384]{2,1,0:T(1,128)S(1)}) custom-call(s32[4]{0:T(128)S(1)} %pad_add_fusion.2.pos_ref, s32[4,4]{1,0:T(4,128)S(1)} %pad_add_fusion.1.lim_ref, bf16[4,128,192]{2,1,0:T(8,128)(2,1)S(1)} %bitcast.350, s32[4,2,128]{2,1,0:T(2,128)S(1)} %pad_add_fusion.rng_ref, ...), custom_call_target="tpu_custom_call" | custom-call | tf_op jit(solution)/shard_map/pallas_call | solution.py:213
  209.3 3.5 convolution_convert_fusion.1
  221.9 3.3 collective-permute-start.30
  227.3 9.3 %collective-permute-done.53 = bf16[4,2,48,1536]{3,2,1,0:T(8,128)(2,1)} collective-permute-done((bf16[4,2,48,1536]{3,2,1,0:T(8,128)(2,1)}, bf16[4,2,48,1536]{3,2,1,0:T(8,128)(2,1)}, u32[]{:S(2)}, u32[]{:S(2)}) %collective-permute-start.53) | collective-permute-done | bytes 1179680 | tf_op jit(solution)/shard_map/ppermute | solution.py:299
  238.2 5.5 %collective-permute-start.54 = (bf16[4,48,1536]{2,1,0:T(8,128)(2,1)S(1)}, bf16[4,48,1536]{2,1,0:T(8,128)(2,1)S(1)}, u32[]{:S(2)}, u32[]{:S(2)}) collective-permute-start(bf16[4,48,1536]{2,1,0:T(8,128)(2,1)S(1)} %dynamic-slice_bitcast_fusion.3), channel_id=1, source_target_pairs={{2,0},{3,1},{0,2},{1,3},{6,4},{7,5},{4,6},{5,7},{10,8},{11,9},{8,1... | collective-permute-start | bytes 1769480 | tf_op jit(solution)/shard_map/ppermute | solution.py:299
  244.8 19.1 %shard_map.272 = (bf16[4,128,192]{2,1,0:T(8,128)(2,1)S(1)}, bf16[32,128,384]{2,1,0:T(8,128)(2,1)S(1)}) custom-call(s32[4]{0:T(128)S(1)} %pad_add_fusion.2.pos_ref, s32[4,4]{1,0:T(4,128)S(1)} %pad_add_fusion.1.lim_ref, bf16[4,128,192]{2,1,0:T(8,128)(2,1)S(1)} %bitcast.351, bf16[4,128,192]{2,1,0:T(8,128)(2,1)S(1)} %pad_maximum_fusion.5.do_ref, ...), custom_call_target="tpu_custom_call" | custom-call | tf_op jit(solution)/shard_map/pallas_call | solution.py:237
  269.6 4.3 %collective-permute-start.48 = (bf16[2,4,120,768]{3,2,1,0:T(8,128)(2,1)}, bf16[2,4,120,768]{3,2,1,0:T(8,128)(2,1)}, u32[]{:S(2)}, u32[]{:S(2)}) collective-permute-start(bf16[2,4,120,768]{3,2,1,0:T(8,128)(2,1)} %fusion.20), channel_id=1, source_target_pairs={{2,0},{3,1},{0,2},{1,3},{6,4},{7,5},{4,6},{5,7},{10,8},{11,9},{8,1... | collective-permute-start | bytes 4423688 | tf_op jit(solution)/shard_map/ppermute | solution.py:299
  273.9 7.8 %collective-permute-done.56 = bf16[48,1536]{1,0:T(8,128)(2,1)S(1)} collective-permute-done((bf16[48,1536]{1,0:T(8,128)(2,1)S(1)}, bf16[48,1536]{1,0:T(8,128)(2,1)S(1)}, u32[]{:S(2)}, u32[]{:S(2)}) %collective-permute-start.56) | collective-permute-done | bytes 147488 | tf_op jit(solution)/shard_map/ppermute | solution.py:299
  284.5 4.4 %collective-permute-start.34 = (bf16[4,128,384]{2,1,0:T(8,128)(2,1)S(1)}, bf16[4,128,384]{2,1,0:T(8,128)(2,1)S(1)}, u32[]{:S(2)}, u32[]{:S(2)}) collective-permute-start(bf16[4,128,384]{2,1,0:T(8,128)(2,1)S(1)} %get-tuple-element.65), channel_id=1, source_target_pairs={{2,0},{3,1},{0,2},{1,3},{6,4},{7,5},{4,6},{5,7},{10,8},{11,9},{8,1... | collective-permute-start | bytes 1179656 | tf_op jit(solution)/shard_map/ppermute | solution.py:299
  291.2 32.2 %collective-permute-done.34 = bf16[4,128,384]{2,1,0:T(8,128)(2,1)S(1)} collective-permute-done((bf16[4,128,384]{2,1,0:T(8,128)(2,1)S(1)}, bf16[4,128,384]{2,1,0:T(8,128)(2,1)S(1)}, u32[]{:S(2)}, u32[]{:S(2)}) %collective-permute-start.34) | collective-permute-done | bytes 393248 | tf_op jit(solution)/shard_map/ppermute | solution.py:299
  330.0 3.4 concatenate.163
  344.3 3.7 collective-permute-start.37
  361.3 3.9 collective-permute-start.45
  365.2 4.5 %collective-permute-done.38 = bf16[128,768]{1,0:T(8,128)(2,1)S(1)} collective-permute-done((bf16[128,768]{1,0:T(8,128)(2,1)S(1)}, bf16[128,768]{1,0:T(8,128)(2,1)S(1)}, u32[]{:S(2)}, u32[]{:S(2)}) %collective-permute-start.38) | collective-permute-done | bytes 196640 | tf_op jit(solution)/shard_map/ppermute | solution.py:299
  371.9 4.2 %collective-permute-done.49 = bf16[4,120,768]{2,1,0:T(8,128)(2,1)S(1)} collective-permute-done((bf16[4,120,768]{2,1,0:T(8,128)(2,1)}, bf16[4,120,768]{2,1,0:T(8,128)(2,1)S(1)}, u32[]{:S(2)}, u32[]{:S(2)}) %collective-permute-start.49) | collective-permute-done | bytes 737312 | tf_op jit(solution)/shard_map/ppermute | solution.py:299
  377.4 3.5 collective-permute-start.50
  386.3 9.5 %collective-permute-done.51 = bf16[120,768]{1,0:T(8,128)(2,1)S(1)} collective-permute-done((bf16[120,768]{1,0:T(8,128)(2,1)S(1)}, bf16[120,768]{1,0:T(8,128)(2,1)S(1)}, u32[]{:S(2)}, u32[]{:S(2)}) %collective-permute-start.51) | collective-permute-done | bytes 184352 | tf_op jit(solution)/shard_map/ppermute | solution.py:299
  (430 shorter events, 167.4 us)
Async XLA Ops:
  13.6 48.9 %collective-permute-start.2 = (bf16[152,768]{1,0:T(8,128)(2,1)}, bf16[152,768]{1,0:T(8,128)(2,1)S(1)}, u32[]{:S(2)}, u32[]{:S(2)}) collective-permute-start(bf16[152,768]{1,0:T(8,128)(2,1)} %get-tuple-element.102), channel_id=1, source_target_pairs={{12,0},{13,1},{14,2},{15,3},{0,4},{1,5},{2,6},{3,7},{4,8},{5,9},{6... | collective-permute-start | bytes 700424 | tf_op jit(solution)/shard_map/ppermute | solution.py:299
  14.8 47.6 %collective-permute-start.1 = (bf16[152,768]{1,0:T(8,128)(2,1)}, bf16[152,768]{1,0:T(8,128)(2,1)S(1)}, u32[]{:S(2)}, u32[]{:S(2)}) collective-permute-start(bf16[152,768]{1,0:T(8,128)(2,1)} %get-tuple-element.103), channel_id=1, source_target_pairs={{8,0},{9,1},{10,2},{11,3},{12,4},{13,5},{14,6},{15,7},{0,8},{1,9},... | collective-permute-start | bytes 700424 | tf_op jit(solution)/shard_map/ppermute | solution.py:299
  15.3 47.2 %collective-permute-start = (bf16[152,768]{1,0:T(8,128)(2,1)S(1)}, bf16[152,768]{1,0:T(8,128)(2,1)S(1)}, u32[]{:S(2)}, u32[]{:S(2)}) collective-permute-start(bf16[152,768]{1,0:T(8,128)(2,1)S(1)} %get-tuple-element.104), channel_id=1, source_target_pairs={{4,0},{5,1},{6,2},{7,3},{8,4},{9,5},{10,6},{11,7},{12,8},{13,9},{1... | collective-permute-start | bytes 700424 | tf_op jit(solution)/shard_map/ppermute | solution.py:299
  21.1 36.5 %collective-permute-start.23 = (bf16[2,24,1536]{2,1,0:T(8,128)(2,1)S(1)}, bf16[2,24,1536]{2,1,0:T(8,128)(2,1)S(1)}, u32[]{:S(2)}, u32[]{:S(2)}) collective-permute-start(bf16[2,24,1536]{2,1,0:T(8,128)(2,1)S(1)} %get-tuple-element.62), channel_id=1, source_target_pairs={{8,0},{9,1},{10,2},{11,3},{12,4},{13,5},{14,6},{15,7},{0,8},{1,9},... | collective-permute-start | bytes 442376 | tf_op jit(solution)/shard_map/ppermute | solution.py:299
  22.0 23.3 %collective-permute-start.22 = (bf16[2,24,1536]{2,1,0:T(8,128)(2,1)S(1)}, bf16[2,24,1536]{2,1,0:T(8,128)(2,1)S(1)}, u32[]{:S(2)}, u32[]{:S(2)}) collective-permute-start(bf16[2,24,1536]{2,1,0:T(8,128)(2,1)S(1)} %get-tuple-element.62), channel_id=1, source_target_pairs={{4,0},{5,1},{6,2},{7,3},{8,4},{9,5},{10,6},{11,7},{12,8},{13,9},{1... | collective-permute-start | bytes 442376 | tf_op jit(solution)/shard_map/ppermute | solution.py:299
  60.9 22.1 %collective-permute-start.25 = (bf16[4,2,24,1536]{3,2,1,0:T(8,128)(2,1)S(1)}, bf16[4,2,24,1536]{3,2,1,0:T(8,128)(2,1)S(1)}, u32[]{:S(2)}, u32[]{:S(2)}) collective-permute-start(bf16[4,2,24,1536]{3,2,1,0:T(8,128)(2,1)S(1)} %constant_dynamic-slice_fusion.1), channel_id=1, source_target_pairs={{16,0},{17,1},{18,2},{19,3},{20,4},{21,5},{22,6},{23,7},{24,8},{25... | collective-permute-start | bytes 1769480 | tf_op jit(solution)/shard_map/ppermute | solution.py:299
  67.1 19.7 %collective-permute-start.17 = (bf16[4,120,768]{2,1,0:T(8,128)(2,1)S(1)}, bf16[4,120,768]{2,1,0:T(8,128)(2,1)S(1)}, u32[]{:S(2)}, u32[]{:S(2)}) collective-permute-start(bf16[4,120,768]{2,1,0:T(8,128)(2,1)S(1)} %fusion.54), channel_id=1, source_target_pairs={{2,0},{3,1},{0,2},{1,3},{6,4},{7,5},{4,6},{5,7},{10,8},{11,9},{8,1... | collective-permute-start | bytes 2211848 | tf_op jit(solution)/shard_map/ppermute | solution.py:299
  85.0 63.8 %collective-permute-start.26 = (bf16[2,4,2,24,1536]{4,3,2,1,0:T(8,128)(2,1)}, bf16[2,4,2,24,1536]{4,3,2,1,0:T(8,128)(2,1)}, u32[]{:S(2)}, u32[]{:S(2)}) collective-permute-start(bf16[2,4,2,24,1536]{4,3,2,1,0:T(8,128)(2,1)} %fusion.31), channel_id=1, source_target_pairs={{2,0},{3,1},{0,2},{1,3},{6,4},{7,5},{4,6},{5,7},{10,8},{11,9},{8,1... | collective-permute-start | bytes 3538952 | tf_op jit(solution)/shard_map/ppermute | solution.py:299
  89.0 55.0 %collective-permute-start.18 = (bf16[2,4,120,768]{3,2,1,0:T(8,128)(2,1)}, bf16[2,4,120,768]{3,2,1,0:T(8,128)(2,1)}, u32[]{:S(2)}, u32[]{:S(2)}) collective-permute-start(bf16[2,4,120,768]{3,2,1,0:T(8,128)(2,1)} %fusion.25), channel_id=1, source_target_pairs={{16,0},{17,1},{18,2},{19,3},{20,4},{21,5},{22,6},{23,7},{24,8},{25... | collective-permute-start | bytes 4423688 | tf_op jit(solution)/shard_map/ppermute | solution.py:299
  95.6 38.3 %collective-permute-start.9 = (bf16[1,4,128,384]{3,2,1,0:T(8,128)(2,1)S(1)}, bf16[1,4,128,384]{3,2,1,0:T(8,128)(2,1)S(1)}, u32[]{:S(2)}, u32[]{:S(2)}) collective-permute-start(bf16[1,4,128,384]{3,2,1,0:T(8,128)(2,1)S(1)} %bitcast.383), channel_id=1, source_target_pairs={{18,0},{19,1},{16,2},{17,3},{22,4},{23,5},{20,6},{21,7},{26,8},{27... | collective-permute-start | bytes 1179656 | tf_op jit(solution)/shard_map/ppermute | solution.py:299
  98.0 41.1 %collective-permute-start.8 = (bf16[1,4,128,384]{3,2,1,0:T(8,128)(2,1)S(1)}, bf16[1,4,128,384]{3,2,1,0:T(8,128)(2,1)S(1)}, u32[]{:S(2)}, u32[]{:S(2)}) collective-permute-start(bf16[1,4,128,384]{3,2,1,0:T(8,128)(2,1)S(1)} %bitcast.384), channel_id=1, source_target_pairs={{16,0},{17,1},{18,2},{19,3},{20,4},{21,5},{22,6},{23,7},{24,8},{25... | collective-permute-start | bytes 1179656 | tf_op jit(solution)/shard_map/ppermute | solution.py:299
  98.6 40.6 %collective-permute-start.7 = (bf16[1,4,128,384]{3,2,1,0:T(8,128)(2,1)S(1)}, bf16[1,4,128,384]{3,2,1,0:T(8,128)(2,1)S(1)}, u32[]{:S(2)}, u32[]{:S(2)}) collective-permute-start(bf16[1,4,128,384]{3,2,1,0:T(8,128)(2,1)S(1)} %bitcast.385), channel_id=1, source_target_pairs={{2,0},{3,1},{0,2},{1,3},{6,4},{7,5},{4,6},{5,7},{10,8},{11,9},{8,1... | collective-permute-start | bytes 1179656 | tf_op jit(solution)/shard_map/ppermute | solution.py:299
  148.7 30.3 %collective-permute-start.19 = (bf16[2,4,2,24,768]{4,3,1,2,0:T(8,128)(2,1)S(1)}, bf16[2,4,2,24,768]{4,3,1,2,0:T(8,128)(2,1)S(1)}, u32[]{:S(2)}, u32[]{:S(2)}) collective-permute-start(bf16[2,4,2,24,768]{4,3,1,2,0:T(8,128)(2,1)S(1)} %get-tuple-element.63), channel_id=1, source_target_pairs={{1,0},{0,1},{3,2},{2,3},{5,4},{4,5},{7,6},{6,7},{9,8},{8,9},{11,10... | collective-permute-start | bytes 1769480 | tf_op jit(solution)/shard_map/ppermute | solution.py:299
  207.9 28.6 %collective-permute-start.53 = (bf16[4,2,48,1536]{3,2,1,0:T(8,128)(2,1)}, bf16[4,2,48,1536]{3,2,1,0:T(8,128)(2,1)}, u32[]{:S(2)}, u32[]{:S(2)}) collective-permute-start(bf16[4,2,48,1536]{3,2,1,0:T(8,128)(2,1)} %dynamic-slice_bitcast_fusion.1), channel_id=1, source_target_pairs={{16,0},{17,1},{18,2},{19,3},{20,4},{21,5},{22,6},{23,7},{24,8},{25... | collective-permute-start | bytes 3538952 | tf_op jit(solution)/shard_map/ppermute | solution.py:299
  221.0 23.7 %collective-permute-start.31 = (bf16[128,192]{1,0:T(8,128)(2,1)S(1)}, bf16[128,192]{1,0:T(8,128)(2,1)S(1)}, u32[]{:S(2)}, u32[]{:S(2)}) collective-permute-start(bf16[128,192]{1,0:T(8,128)(2,1)S(1)} %get-tuple-element.95), channel_id=1, source_target_pairs={{8,0},{9,1},{10,2},{11,3},{12,4},{13,5},{14,6},{15,7},{0,8},{1,9},... | collective-permute-start | bytes 147464 | tf_op jit(solution)/shard_map/ppermute | solution.py:299
  221.9 22.8 %collective-permute-start.30 = (bf16[128,192]{1,0:T(8,128)(2,1)S(1)}, bf16[128,192]{1,0:T(8,128)(2,1)S(1)}, u32[]{:S(2)}, u32[]{:S(2)}) collective-permute-start(bf16[128,192]{1,0:T(8,128)(2,1)S(1)} %get-tuple-element.96), channel_id=1, source_target_pairs={{4,0},{5,1},{6,2},{7,3},{8,4},{9,5},{10,6},{11,7},{12,8},{13,9},{1... | collective-permute-start | bytes 147464 | tf_op jit(solution)/shard_map/ppermute | solution.py:299
  225.2 19.5 %collective-permute-start.32 = (bf16[128,192]{1,0:T(8,128)(2,1)S(1)}, bf16[128,192]{1,0:T(8,128)(2,1)S(1)}, u32[]{:S(2)}, u32[]{:S(2)}) collective-permute-start(bf16[128,192]{1,0:T(8,128)(2,1)S(1)} %get-tuple-element.97), channel_id=1, source_target_pairs={{12,0},{13,1},{14,2},{15,3},{0,4},{1,5},{2,6},{3,7},{4,8},{5,9},{6... | collective-permute-start | bytes 147464 | tf_op jit(solution)/shard_map/ppermute | solution.py:299
  227.2 37.0 %collective-permute-start.47 = (bf16[2,4,2,24,768]{4,3,2,1,0:T(8,128)(2,1)S(1)}, bf16[2,4,2,24,768]{4,3,2,1,0:T(8,128)(2,1)S(1)}, u32[]{:S(2)}, u32[]{:S(2)}) collective-permute-start(bf16[2,4,2,24,768]{4,3,2,1,0:T(8,128)(2,1)S(1)} %fusion.58), channel_id=1, source_target_pairs={{1,0},{0,1},{3,2},{2,3},{5,4},{4,5},{7,6},{6,7},{9,8},{8,9},{11,10... | collective-permute-start | bytes 1769480 | tf_op jit(solution)/shard_map/ppermute | solution.py:299
  238.2 26.1 %collective-permute-start.54 = (bf16[4,48,1536]{2,1,0:T(8,128)(2,1)S(1)}, bf16[4,48,1536]{2,1,0:T(8,128)(2,1)S(1)}, u32[]{:S(2)}, u32[]{:S(2)}) collective-permute-start(bf16[4,48,1536]{2,1,0:T(8,128)(2,1)S(1)} %dynamic-slice_bitcast_fusion.3), channel_id=1, source_target_pairs={{2,0},{3,1},{0,2},{1,3},{6,4},{7,5},{4,6},{5,7},{10,8},{11,9},{8,1... | collective-permute-start | bytes 1769480 | tf_op jit(solution)/shard_map/ppermute | solution.py:299
  264.1 18.5 %collective-permute-start.33 = (bf16[4,2,2,128,384]{4,3,2,1,0:T(8,128)(2,1)S(1)}, bf16[4,2,2,128,384]{4,3,2,1,0:T(8,128)(2,1)S(1)}, u32[]{:S(2)}, u32[]{:S(2)}) collective-permute-start(bf16[4,2,2,128,384]{4,3,2,1,0:T(8,128)(2,1)S(1)} %dynamic-slice_bitcast_fusion), channel_id=1, source_target_pairs={{1,0},{0,1},{3,2},{2,3},{5,4},{4,5},{7,6},{6,7},{9,8},{8,9},{11,10... | collective-permute-start | bytes 4718600 | tf_op jit(solution)/shard_map/ppermute | solution.py:299
  269.6 81.9 %collective-permute-start.48 = (bf16[2,4,120,768]{3,2,1,0:T(8,128)(2,1)}, bf16[2,4,120,768]{3,2,1,0:T(8,128)(2,1)}, u32[]{:S(2)}, u32[]{:S(2)}) collective-permute-start(bf16[2,4,120,768]{3,2,1,0:T(8,128)(2,1)} %fusion.20), channel_id=1, source_target_pairs={{2,0},{3,1},{0,2},{1,3},{6,4},{7,5},{4,6},{5,7},{10,8},{11,9},{8,1... | collective-permute-start | bytes 4423688 | tf_op jit(solution)/shard_map/ppermute | solution.py:299
  284.5 38.8 %collective-permute-start.34 = (bf16[4,128,384]{2,1,0:T(8,128)(2,1)S(1)}, bf16[4,128,384]{2,1,0:T(8,128)(2,1)S(1)}, u32[]{:S(2)}, u32[]{:S(2)}) collective-permute-start(bf16[4,128,384]{2,1,0:T(8,128)(2,1)S(1)} %get-tuple-element.65), channel_id=1, source_target_pairs={{2,0},{3,1},{0,2},{1,3},{6,4},{7,5},{4,6},{5,7},{10,8},{11,9},{8,1... | collective-permute-start | bytes 1179656 | tf_op jit(solution)/shard_map/ppermute | solution.py:299
  288.9 34.4 %collective-permute-start.36 = (bf16[4,128,384]{2,1,0:T(8,128)(2,1)S(1)}, bf16[4,128,384]{2,1,0:T(8,128)(2,1)S(1)}, u32[]{:S(2)}, u32[]{:S(2)}) collective-permute-start(bf16[4,128,384]{2,1,0:T(8,128)(2,1)S(1)} %get-tuple-element.66), channel_id=1, source_target_pairs={{18,0},{19,1},{16,2},{17,3},{22,4},{23,5},{20,6},{21,7},{26,8},{27... | collective-permute-start | bytes 1179656 | tf_op jit(solution)/shard_map/ppermute | solution.py:299
  288.9 34.4 %collective-permute-start.35 = (bf16[4,128,384]{2,1,0:T(8,128)(2,1)S(1)}, bf16[4,128,384]{2,1,0:T(8,128)(2,1)S(1)}, u32[]{:S(2)}, u32[]{:S(2)}) collective-permute-start(bf16[4,128,384]{2,1,0:T(8,128)(2,1)S(1)} %get-tuple-element.67), channel_id=1, source_target_pairs={{16,0},{17,1},{18,2},{19,3},{20,4},{21,5},{22,6},{23,7},{24,8},{25... | collective-permute-start | bytes 1179656 | tf_op jit(solution)/shard_map/ppermute | solution.py:299
  (94 other events, 841.4 us)
